TPU v7x, 128 devices: a whole 4x4x4 slice. The times are simulated.
128 devices in a mesh: dp: 8 (over x, y_lo), fsdp: 16 (over y_hi, z, core).
Axes of the slice: x: 4, y: 4 (y_hi: 2, y_lo: 2; y = y_hi * 2 + y_lo), z: 4, core: 2. Of those that a mesh axis runs over, the one named last changes fastest.
Arguments:
- tokens: float32 [131072, 4096], P(('dp', 'fsdp')), may hold values from -6 to 6
- curvature: float32 [131072, 512], P(('dp', 'fsdp')), may hold values from 0.05 to 1
- values: float32 [4096, 512], P('fsdp'), may hold values from -6 to 6
- input_basis: float32 [4096, 4096], P(None, ('dp', 'fsdp')), may hold values from -1 to 1, as said below
- output_basis: float32 [512, 512], replicated, may hold values from -1 to 1, as said below
- eigenvalues: float32 [4096, 512], P(('dp', 'fsdp')), may hold values from 0.3 to 3
Outputs:
- stepped: float32 [4096, 512], P('fsdp')
Inputs may be any that keep to these rules, and one draw needn't show every extreme that they name: `input_basis`: an orthogonal 4096 x 4096 matrix. `output_basis`: an orthogonal 512 x 512 matrix.
All inputs are finite; a program needn't handle non-finite values.
Results may differ from a plain program's by a relative error of at most 0.000071.
Values sent between devices are 32-bit elements; how exact they have to be, the bound alone decides.
A program may use at most 128 MiB of HBM per device.

v0:
```python
import jax
import jax.numpy as jnp
from jax import lax
from jax.sharding import PartitionSpec as P


def body(tokens, curvature, values, input_basis, output_basis, eigenvalues):
    highest = lax.Precision.HIGHEST
    local_tokens = tokens.shape[0]
    inverse_total = 1.0 / (local_tokens * lax.axis_size("dp") * lax.axis_size("fsdp"))
    columns = tokens
    projected = jnp.dot(
        columns,
        lax.all_gather(values, "fsdp", axis=0, tiled=True),
        precision=highest,
        preferred_element_type=jnp.float32,
    )
    weighted = curvature * projected
    columns = tokens
    product = lax.dot_general(
        columns,
        weighted,
        (((0,), (0,)), ((), ())),
        precision=highest,
        preferred_element_type=jnp.float32,
    )
    group_rows = lax.psum_scatter(product * inverse_total, "fsdp", scatter_dimension=0, tiled=True)
    summed_rows = lax.psum(group_rows, "dp")
    basis_rows = input_basis
    left_rotated = lax.dot_general(
        basis_rows,
        lax.all_gather(summed_rows, "fsdp", axis=0, tiled=True),
        (((0,), (0,)), ((), ())),
        precision=highest,
        preferred_element_type=jnp.float32,
    )
    rotated = jnp.dot(
        left_rotated, output_basis, precision=highest, preferred_element_type=jnp.float32
    )
    scaled = rotated / eigenvalues
    mapped = lax.dot_general(
        scaled,
        output_basis,
        (((1,), (1,)), ((), ())),
        precision=highest,
        preferred_element_type=jnp.float32,
    )
    basis_rows = input_basis
    update_part = lax.psum_scatter(
        jnp.dot(basis_rows, mapped, precision=highest, preferred_element_type=jnp.float32),
        "fsdp",
        scatter_dimension=0,
        tiled=True,
    )
    update = lax.psum(update_part, "dp")
    return values - update


def solution(mesh):
    placed = (
        P(("dp", "fsdp"), None),
        P(("dp", "fsdp"), None),
        P("fsdp", None),
        P(None, ("dp", "fsdp")),
        P(),
        P(("dp", "fsdp"), None),
    )
    return jax.shard_map(
        body, mesh=mesh, in_specs=placed, out_specs=P("fsdp", None), check_vma=False
    )
```

profile of v0, /device:TPU:0, one launch (start us, length us, event | category | flops | bytes accessed | tf_op | source)
XLA Modules:
  0.0 606.2 jit_solution(12661123287436959348)
XLA Ops:
  6.5 0.0 copy-start
  6.5 0.0 all-gather.3.cloned.1.call-start
  6.5 0.7 all-gather.3.cloned.1.call-update
  7.3 0.0 copy-start.1
  7.3 0.0 reduce-scatter.3.cloned.1.call-start
  7.3 78.2 %all-gather.3.cloned.1.call-done = f32[4096,512]{1,0:T(8,128)} async-done(((f32[256,512]{1,0:T(8,128)}), f32[4096,512]{1,0:T(8,128)}) %all-gather.3.cloned.1.call-update) | async-done | bytes 8388624 | tf_op jit(solution)/shard_map/all_gather | solution.py:14
  85.5 29.9 %fusion.1 = f32[1024,512]{1,0:T(8,128)S(1)} fusion(f32[1024,4096]{1,0:T(8,128)} %param.6, f32[4096,512]{1,0:T(8,128)} %all-gather.3.cloned.1.call-done), kind=kOutput, calls=%fused_computation.4 | convolution fusion | flops 25769803776 | bytes 27262976 | tf_op jit(solution)/shard_map/dot_general | solution.py:12
  115.4 0.0 copy-done.1
  115.4 31.3 %multiply_bitcast_fusion = f32[4096,512]{0,1:T(8,128)} fusion(f32[1024,4096]{1,0:T(8,128)} %param.6, f32[1024,512]{1,0:T(8,128)S(1)} %copy-done.1, f32[1024,512]{1,0:T(8,128)S(1)} %fusion.1), kind=kOutput, calls=%fused_computation | convolution fusion | flops 25772425216 | bytes 29360128 | tf_op jit(solution)/shard_map/dot_general | solution.py:20
  146.6 0.0 copy-start.2
  146.6 0.0 copy-start.4
  146.6 0.0 reduce-scatter.3.cloned.1.call-update
  146.6 0.0 all-reduce.3.cloned.1.call-start
  146.7 100.2 %reduce-scatter.3.cloned.1.call-done = f32[256,512]{0,1:T(8,128)} async-done(((f32[4096,512]{0,1:T(8,128)}), f32[256,512]{0,1:T(8,128)}) %reduce-scatter.3.cloned.1.call-update) | async-done | bytes 524304 | tf_op jit(solution)/shard_map/reduce_scatter | solution.py:27
  246.9 0.0 all-reduce.3.cloned.1.call-update
  246.9 0.0 all-gather.5.cloned.1.call-start
  247.0 75.6 %all-reduce.3.cloned.1.call-done = f32[256,512]{0,1:T(8,128)} async-done(((f32[256,512]{0,1:T(8,128)}), f32[256,512]{0,1:T(8,128)}) %all-reduce.3.cloned.1.call-update) | async-done | bytes 524304 | tf_op jit(solution)/shard_map/psum | solution.py:28
  322.6 0.0 all-gather.5.cloned.1.call-update
  322.6 0.0 reduce-scatter.5.cloned.1.call-start
  322.7 79.0 %all-gather.5.cloned.1.call-done = f32[4096,512]{0,1:T(8,128)} async-done(((f32[256,512]{0,1:T(8,128)}), f32[4096,512]{0,1:T(8,128)}) %all-gather.5.cloned.1.call-update) | async-done | bytes 8388624 | tf_op jit(solution)/shard_map/all_gather | solution.py:32
  401.6 0.0 copy-done.2
  401.6 9.0 %fusion.2 = f32[512,32]{1,0:T(8,128)S(1)} fusion(f32[4096,512]{0,1:T(8,128)} %all-gather.5.cloned.1.call-done, f32[4096,32]{0,1:T(8,128)S(1)} %copy-done.2), kind=kOutput, calls=%fused_computation.5 | convolution fusion | flops 805306368 | bytes 8978432 | tf_op jit(solution)/shard_map/dot_general | solution.py:30
  410.6 0.0 copy-done
  410.6 0.0 copy-done.4
  410.6 0.7 convolution_divide_fusion
  411.4 1.0 fusion.3
  412.4 0.0 copy-start.3
  412.4 8.9 %convolution_bitcast_fusion = f32[4096,512]{0,1:T(8,128)} fusion(f32[32,512]{1,0:T(8,128)S(1)} %fusion.3, f32[4096,32]{0,1:T(8,128)S(1)} %copy-done.2), kind=kOutput, calls=%fused_computation.1 | convolution fusion | flops 805306368 | bytes 8978432 | tf_op jit(solution)/shard_map/dot_general | solution.py:50
  421.4 0.0 reduce-scatter.5.cloned.1.call-update
  421.4 0.0 all-reduce.5.cloned.1.call-start
  421.5 100.0 %reduce-scatter.5.cloned.1.call-done = f32[256,512]{0,1:T(8,128)} async-done(((f32[4096,512]{0,1:T(8,128)}), f32[256,512]{0,1:T(8,128)}) %reduce-scatter.5.cloned.1.call-update) | async-done | bytes 524304 | tf_op jit(solution)/shard_map/reduce_scatter | solution.py:49
  521.4 0.0 all-reduce.5.cloned.1.call-update
  521.5 0.0 copy-done.3
  521.5 0.2 copy.7
  521.7 75.6 %all-reduce.5.cloned.1.call-done = f32[256,512]{0,1:T(8,128)} async-done(((f32[256,512]{0,1:T(8,128)}), f32[256,512]{0,1:T(8,128)}) %all-reduce.5.cloned.1.call-update) | async-done | bytes 524304 | tf_op jit(solution)/shard_map/psum | solution.py:55
  597.3 1.1 sub.3
  598.4 1.0 copy.8
Async XLA Ops:
  6.5 404.1 %copy-start = (f32[512,512]{1,0:T(8,128)S(1)}, f32[512,512]{1,0:T(8,128)}, u32[]{:S(2)}) copy-start(f32[512,512]{1,0:T(8,128)} %param.10) | copy-start | bytes 3145732
  6.5 78.9 %all-gather.3.cloned.1.call-start = ((), (), s32[]{:S(2)}) async-start(), calls=%async_computation.2 | async-start | bytes 8912896 | tf_op jit(solution)/shard_map/all_gather | solution.py:14
  7.3 108.1 %copy-start.1 = (f32[1024,512]{1,0:T(8,128)S(1)}, f32[1024,512]{1,0:T(8,128)}, u32[]{:S(2)}) copy-start(f32[1024,512]{1,0:T(8,128)} %param.7) | copy-start | bytes 6291460
  7.3 239.7 %reduce-scatter.3.cloned.1.call-start = ((), (), s32[]{:S(2)}) async-start(), calls=%async_computation.3 | async-start | bytes 8912896 | tf_op jit(solution)/shard_map/reduce_scatter | solution.py:27
  146.6 255.0 %copy-start.2 = (f32[4096,32]{0,1:T(8,128)S(1)}, f32[4096,32]{0,1:T(8,128)}, u32[]{:S(2)}) copy-start(f32[4096,32]{0,1:T(8,128)} %param.9) | copy-start | bytes 1572868
  146.6 264.0 %copy-start.4 = (f32[32,512]{1,0:T(8,128)S(1)}, f32[32,512]{1,0:T(8,128)}, u32[]{:S(2)}) copy-start(f32[32,512]{1,0:T(8,128)} %param.11) | copy-start | bytes 196612
  146.6 175.9 %all-reduce.3.cloned.1.call-start = ((), (), s32[]{:S(2)}) async-start(), calls=%async_computation.4 | async-start | bytes 1048576 | tf_op jit(solution)/shard_map/psum | solution.py:28
  246.9 154.7 %all-gather.5.cloned.1.call-start = ((), (), s32[]{:S(2)}) async-start(), calls=%async_computation.5 | async-start | bytes 8912896 | tf_op jit(solution)/shard_map/all_gather | solution.py:32
  322.6 198.8 %reduce-scatter.5.cloned.1.call-start = ((), (), s32[]{:S(2)}) async-start(), calls=%async_computation.6 | async-start | bytes 8912896 | tf_op jit(solution)/shard_map/reduce_scatter | solution.py:49
  412.4 109.0 %copy-start.3 = (f32[256,512]{1,0:T(8,128)S(1)}, f32[256,512]{1,0:T(8,128)}, u32[]{:S(2)}) copy-start(f32[256,512]{1,0:T(8,128)} %param.8) | copy-start | bytes 1572868
  421.4 175.9 %all-reduce.5.cloned.1.call-start = ((), (), s32[]{:S(2)}) async-start(), calls=%async_computation.7 | async-start | bytes 1048576 | tf_op jit(solution)/shard_map/psum | solution.py:55
Sparse Core Ops, SparseCore 0:
  9.8 75.5 all-gather.2
  146.8 100.1 reduce-scatter.2
  249.4 73.1 all-reduce.2
  325.0 76.6 all-gather.4
  421.5 99.8 reduce-scatter.4
  523.9 73.2 all-reduce.4
where the time goes:
time: 606 us
  waiting for transfers between devices  509 us (84%)
  matrix products  80.8 us (13%)
  between operations  13.6 us (2%)
    reduce_scatter x1, waiting for transfers between devices, body(): lax.psum_scatter(product * inverse_total, 'fsdp', scatter_dimension=0, ti...  100 us
    reduce_scatter x1, waiting for transfers between devices, body(): lax.psum_scatter(jnp.dot(basis_rows, mapped, precision=highest, preferred...  100 us
    all_gather x1, waiting for transfers between devices, body(): lax.all_gather(summed_rows, 'fsdp', axis=0, tiled=True)  79 us
    all_gather x1, waiting for transfers between devices, body(): lax.all_gather(values, 'fsdp', axis=0, tiled=True)  78.2 us
    psum x1, waiting for transfers between devices, body(): summed_rows = lax.psum(group_rows, 'dp')  75.6 us
    psum x1, waiting for transfers between devices, body(): update = lax.psum(update_part, 'dp')  75.6 us
    dot_general x1, matrix products, body(): lax.dot_general(columns, weighted, (((0,), (0,)), ((), ())), precision=hi...  31.3 us
    dot_general x1, matrix products, body(): jnp.dot(columns, lax.all_gather(values, 'fsdp', axis=0, tiled=True), prec...  29.9 us
  transfers between devices with their start and end apart: 6, of which 6 were waited for; matrix products, arithmetic and copies ran while one was open for 0% of the time, Pallas kernels for 0%

commit v1 on v0

v1 whole, which is shorter than its diff:
```python
import functools

import jax
import jax.numpy as jnp
from jax import lax
from jax.experimental import pallas as pl
from jax.experimental.pallas import tpu as pltpu
from jax.sharding import PartitionSpec as P

F32 = jnp.float32
BF16 = jnp.bfloat16
MESH = pl.DeviceIdType.MESH
ALL = slice(None)

ORDERS = (("z", "y", "x"), ("y", "x", "z"), ("x", "z", "y"))
ROWS = ((0, 24), (24, 48), (48, 64))


def split(v):
    hi = v.astype(BF16)
    return hi, (v - hi.astype(F32)).astype(BF16)


def mm(a, b, dims=(((1,), (0,)), ((), ()))):
    return lax.dot_general(a, b, dims, preferred_element_type=F32)


NT = (((1,), (1,)), ((), ()))


def mm3(ah, al, bh, bl, dims=(((1,), (0,)), ((), ()))):
    return mm(ah, bh, dims) + (mm(ah, bl, dims) + mm(al, bh, dims))


def half_shape(o, p):
    lo, hi = ROWS[o]
    rows = hi - lo
    r_axis = ORDERS[o][2]
    if p == 2:
        return (16, 128)
    if p == 1:
        return (2, rows, 128)
    q_axis = ORDERS[o][1]
    dims = [a for a in "zyx" if a in (q_axis, r_axis)]
    return tuple(2 if a == r_axis else 4 for a in dims) + (rows, 128)


def full_shape(o, p):
    lo, hi = ROWS[o]
    return ((4, 4), (4,), ())[p] + (hi - lo, 128)


def kernel(tok, curv, val, ut, ot, outb, eig, out, *scr, inverse_total):
    (V, thi, tlo, stage, cv, acc, whi, wlo, zhi, zlo, sib, mg, utg, uhi, ulo, eg, ub, ubr, rb, ud,
     *rest) = scr
    RH = [[rest[o * 3 + p] for p in range(3)] for o in range(3)]
    RF = [[rest[9 + o * 3 + p] for p in range(3)] for o in range(3)]
    (ag_s, ag_r, fw_s, fw_r, u_s, u_r, e_s, e_r, sb_s, sb_r, rs_s, rs_r,
     mg_s, mg_r, ub_s, ub_r, ud_s, ud_r, st_sem, lc_sem) = rest[18:]

    dp = lax.axis_index("dp")
    fs = lax.axis_index("fsdp")
    x, ylo = lax.div(dp, 2), lax.rem(dp, 2)
    yhi, z, c = lax.div(fs, 8), lax.rem(lax.div(fs, 2), 4), lax.rem(fs, 2)
    y = yhi * 2 + ylo
    pos = {"x": x, "y": y, "z": z}

    def dev(x_, y_, z_, c_):
        return (x_ * 2 + lax.rem(y_, 2), lax.div(y_, 2) * 8 + z_ * 2 + c_)

    def off(v, d):
        return lax.rem(v + (d + 4), 4)

    def nb(axis, d):
        q = dict(pos)
        q[axis] = off(q[axis], d)
        return dev(q["x"], q["y"], q["z"], c)

    sibling = dev(x, y, z, 1 - c)

    def rc(src, dst, ss, rs, to):
        return pltpu.make_async_remote_copy(
            src_ref=src, dst_ref=dst, send_sem=ss, recv_sem=rs, device_id=to, device_id_type=MESH)

    def block_index(o, axis_idx, rows):
        lo, hi = ROWS[o]
        if rows is None:
            rows = (lo, hi)
        return (axis_idx["z"], axis_idx["y"], axis_idx["x"], slice(*rows))

    def grid_index(o, lead, k, half):
        axes = ORDERS[o]
        idx = {a: pos[a] for a in axes[:lead]}
        idx[axes[lead]] = k
        for a in axes[lead + 1:]:
            idx[a] = ALL
        rows = None
        if half is not None:
            if lead == 2:
                lo, hi = ROWS[o]
                mid = lo + (16 if hi - lo == 24 else 8)
                rows = (lo, mid) if half == 0 else (mid, hi)
            else:
                idx[axes[2]] = slice(0, 2) if half == 0 else slice(2, 4)
        return block_index(o, idx, rows)

    def vidx(r, cc, g):
        return (r, g[0], cc, g[1], g[2], g[3], ALL)

    def ag_copy(r, o, p, k):
        lead = 2 - p
        axis = ORDERS[o][lead]
        me = pos[axis]
        i = ((r * 3 + o) * 3 + p) * 4 + k
        if k == 0:
            g, to = grid_index(o, lead, me, None), nb(axis, 1)
        elif k == 1:
            g, to = grid_index(o, lead, me, None), nb(axis, -1)
        elif k == 2:
            g, to = grid_index(o, lead, off(me, -1), 0), nb(axis, 1)
        else:
            g, to = grid_index(o, lead, off(me, 1), 1), nb(axis, -1)
        ref = V.at[vidx(r, c, g)]
        return rc(ref, ref, ag_s.at[i], ag_r.at[i], to)

    def fw_copy(r, o, d):
        me = pos[ORDERS[o][0]]
        ref = V.at[vidx(r, c, grid_index(o, 0, off(me, d), None))]
        i = (r * 3 + o) * 4 + (d + 4) % 4
        return rc(ref, ref, fw_s.at[i], fw_r.at[i], sibling)

    def ag_start(r, p):
        for o in range(3):
            ag_copy(r, o, p, 0).start()
            ag_copy(r, o, p, 1).start()
            if p == 2:
                fw_copy(r, o, 0).start()

    def ag_relay(r, p):
        for o in range(3):
            ag_copy(r, o, p, 0).wait_recv()
            ag_copy(r, o, p, 2).start()
            ag_copy(r, o, p, 1).wait_recv()
            ag_copy(r, o, p, 3).start()
            if p == 2:
                fw_copy(r, o, -1).start()
                fw_copy(r, o, 1).start()

    def ag_finish(r, p):
        for o in range(3):
            ag_copy(r, o, p, 2).wait_recv()
            ag_copy(r, o, p, 3).wait_recv()
            if p == 2:
                fw_copy(r, o, 2).start()

    def fw_wait(r):
        for o in range(3):
            for d in (0, -1, 1, 2):
                fw_copy(r, o, d).wait_recv()

    def ag_sent(r):
        for o in range(3):
            for p in range(3):
                for k in range(4):
                    ag_copy(r, o, p, k).wait_send()
            for d in (0, -1, 1, 2):
                fw_copy(r, o, d).wait_send()

    def u_copy(k):
        i, to, rows = ((x, nb("x", 1), ALL), (x, nb("x", -1), ALL),
                       (off(x, -1), nb("x", 1), slice(0, 16)), (off(x, 1), nb("x", -1), slice(16, 32)))[k]
        ref = utg.at[i, rows, :]
        return rc(ref, ref, u_s.at[k], u_r.at[k], to)

    def e_copy(d):
        xt = off(x, d)
        cols = pl.ds(pl.multiple_of(xt * 128, 128), 128)
        return rc(eig.at[:, cols], eg.at[x], e_s.at[d - 1], e_r.at[d - 1], dev(xt, y, z, c))

    def sb_copy(s, zi):
        return rc(V.at[s, zi, 1 - c], sib.at[s, zi], sb_s.at[s * 4 + zi], sb_r.at[s * 4 + zi], sibling)

    def rh_view(s, o, p, d):
        ref = RH[o][p]
        if p == 2:
            lo, hi = ROWS[o]
            first = 16 if hi - lo == 24 else 8
            n = first if d == 0 else hi - lo - first
            return (s, d, slice(0, n), ALL), ref
        return (s, d), ref

    def rs_copy(s, o, p, k):
        axis = ORDERS[o][p]
        me = pos[axis]
        i = ((s * 3 + o) * 3 + p) * 4 + k
        d = k % 2
        to = nb(axis, 1 if d == 0 else -1)
        if k < 2:
            g = grid_index(o, p, off(me, 2), d)
            idx, ref = rh_view(s, o, p, d)
            dst = ref.at[idx]
        else:
            g = grid_index(o, p, off(me, 1 if d == 0 else -1), None)
            dst = RF[o][p].at[s, d]
        return rc(V.at[vidx(s, c, g)], dst, rs_s.at[i], rs_r.at[i], to)

    def rs_start(s, p):
        for o in range(3):
            rs_copy(s, o, p, 0).start()
            rs_copy(s, o, p, 1).start()

    def rs_mid(s, p):
        for o in range(3):
            me = pos[ORDERS[o][p]]
            for d, k in ((0, off(me, 1)), (1, off(me, -1))):
                rs_copy(s, o, p, d).wait_recv()
                idx, ref = rh_view(s, o, p, d)
                v = vidx(s, c, grid_index(o, p, k, d))
                V[v] = V[v] + ref[idx]
                rs_copy(s, o, p, 2 + d).start()

    def rs_end(s, p):
        for o in range(3):
            me = pos[ORDERS[o][p]]
            rs_copy(s, o, p, 2).wait_recv()
            rs_copy(s, o, p, 3).wait_recv()
            v = vidx(s, c, grid_index(o, p, me, None))
            V[v] = V[v] + (RF[o][p][s, 0] + RF[o][p][s, 1])

    def sib_add(s):
        def one(zi, _):
            sb_copy(s, zi).wait_recv()
            for yi in range(4):
                V[s, zi, c, yi] = V[s, zi, c, yi] + sib[s, zi, yi]
            return 0
        lax.fori_loop(0, 4, one, 0)

    def peer(k):
        return off(y, 0 + lax.div(k, 4)), off(z, 0 + lax.rem(k, 4))

    def mg_copy(s, k):
        yt, zt = peer(k)
        i = s * 16 + k
        return rc(V.at[s, z, c, y, x], mg.at[s, c, y, z], mg_s.at[i], mg_r.at[i], dev(x, yt, zt, c))

    def mg_fwd(s):
        return rc(mg.at[s, c], mg.at[s, c], mg_s.at[s * 16], mg_r.at[s * 16], sibling)

    def ub_copy(s, k):
        yt, zt = peer(k)
        i = s * 16 + k
        return rc(ub.at[s, c, yt, zt], rb.at[s, k], ub_s.at[i], ub_r.at[i], dev(x, yt, zt, c))

    def ub_sib(s):
        return rc(ub.at[s, 1 - c], ubr.at[s], ub_s.at[s * 16], ub_r.at[s * 16], sibling)

    def ud_copy(s, k):
        xt = off(x, lax.div(k, 2))
        lt = lax.rem(ylo + lax.rem(k, 2), 2)
        i = s * 8 + k
        return rc(ud.at[s, x, ylo], ud.at[s, x, ylo], ud_s.at[i], ud_r.at[i], dev(xt, yhi * 2 + lt, z, c))

    def loop(lo, hi, f):
        def step(i, carry):
            f(i)
            return carry
        lax.fori_loop(lo, hi, step, 0)

    def t_copy(j, slot):
        cols = pl.ds(pl.multiple_of(j * 256, 256), 256)
        return pltpu.make_async_copy(tok.at[:, cols], stage.at[slot], st_sem.at[slot])

    t_copy(0, 0).start()
    t_copy(1, 1).start()
    own = []
    for yl in range(2):
        for r in range(2):
            pass
    val_copies = []
    rowbase = pl.multiple_of(x * 64, 64)
    colbase = pl.multiple_of(ylo * 128, 128)
    for r in range(2):
        cols = pl.ds(pl.multiple_of(colbase + r * 256, 128), 128)
        val_copies.append(pltpu.make_async_copy(
            val.at[pl.ds(rowbase, 64), cols], V.at[r, z, c, y, x], lc_sem.at[r]))
        val_copies[-1].start()
    cv_copy = pltpu.make_async_copy(curv, cv, lc_sem.at[2])
    cv_copy.start()
    ut_copy = pltpu.make_async_copy(ut, utg.at[x], lc_sem.at[3])
    ut_copy.start()

    barrier = pltpu.get_barrier_semaphore()
    loop(1, 16, lambda k: pl.semaphore_signal(
        barrier, inc=1, device_id=dev(x, *peer(k), c), device_id_type=MESH))

    def greet_dp(k):
        xt = off(x, lax.div(k, 2))
        lt = lax.rem(ylo + lax.rem(k, 2), 2)
        pl.semaphore_signal(barrier, inc=1, device_id=dev(xt, yhi * 2 + lt, z, c), device_id_type=MESH)
    loop(2, 8, greet_dp)
    pl.semaphore_signal(barrier, inc=1, device_id=sibling, device_id_type=MESH)
    pl.semaphore_wait(barrier, 22)

    for cp in val_copies:
        cp.wait()

    def split_block(j):
        slot = lax.rem(j, 2)
        t_copy(j, slot).wait()
        kb = lax.div(j, 2)
        cols = pl.ds(pl.multiple_of(lax.rem(j, 2) * 256, 256), 256)

        def rows(i):
            rr = pl.ds(pl.multiple_of(i * 256, 256), 256)
            h, l = split(stage[slot, rr, :])
            thi[kb, rr, cols] = h
            tlo[kb, rr, cols] = l
        loop(0, 4, rows)

        @pl.when(j < 14)
        def _():
            t_copy(j + 2, slot).start()

    ag_start(0, 0)
    ag_start(1, 0)
    loop(0, 2, split_block)
    ag_relay(0, 0)
    ag_relay(1, 0)
    loop(2, 4, split_block)
    ag_finish(0, 0)
    ag_start(0, 1)
    ag_finish(1, 0)
    ag_start(1, 1)
    loop(4, 7, split_block)
    ag_relay(0, 1)
    ag_relay(1, 1)
    loop(7, 9, split_block)
    ag_finish(0, 1)
    ag_start(0, 2)
    ag_finish(1, 1)
    loop(9, 14, split_block)
    ag_relay(0, 2)
    ag_start(1, 2)
    loop(14, 16, split_block)
    ag_finish(0, 2)
    ut_copy.wait()
    u_copy(0).start()
    u_copy(1).start()
    for d in (1, 2, 3):
        e_copy(d).start()
    eg[x] = eig[:, pl.ds(pl.multiple_of(x * 128, 128), 128)]
    cv_copy.wait()
    fw_wait(0)

    def project(r, steps):
        def body(kb):
            for at, fn in steps:
                pl.when(kb == at)(fn)
            yh, zi = lax.div(kb, 4), lax.rem(kb, 4)
            rows = []
            for ci in range(2):
                tiles = [V[r, zi, ci, yh * 2 + yl].reshape(256, 128) for yl in range(2)]
                rows.append(jnp.concatenate(tiles, axis=1))
            vh, vl = split(jnp.concatenate(rows, axis=0))
            for m in range(2):
                rr = slice(m * 512, (m + 1) * 512)
                part = mm3(thi[kb, rr, :], tlo[kb, rr, :], vh, vl)

                @pl.when(kb == 0)
                def _():
                    acc[rr, :] = part

                @pl.when(kb > 0)
                def _():
                    acc[rr, :] = acc[rr, :] + part
        loop(0, 8, body)

        def weigh(i):
            rr = pl.ds(pl.multiple_of(i * 256, 256), 256)
            cols = slice(r * 256, (r + 1) * 256)
            h, l = split(cv[rr, cols] * acc[rr, :] * inverse_total)
            whi[rr, cols] = h
            wlo[rr, cols] = l
        loop(0, 4, weigh)

    def u_relay():
        u_copy(0).wait_recv()
        u_copy(2).start()
        u_copy(1).wait_recv()
        u_copy(3).start()

    project(0, [(6, lambda: ag_relay(1, 2))])
    ag_finish(1, 2)
    fw_wait(1)
    project(1, [(6, u_relay)])
    ag_sent(0)
    ag_sent(1)

    for s in range(2):
        oh, ol = split(ot[:, s].reshape(256, 512))

        def z_part(i):
            rr = pl.ds(pl.multiple_of(i * 256, 256), 256)
            zz = mm3(oh, ol, whi[rr, :], wlo[rr, :], NT)
            h, l = split(zz)
            zhi[s, :, rr] = h
            zlo[s, :, rr] = l
        loop(0, 4, z_part)

    def moment(s, steps):
        def body(i):
            for at, fn in steps:
                pl.when(i == at)(fn)
            zi, yh = lax.div(i, 2), lax.rem(i, 2)
            kb = yh * 4 + zi
            mo = mm3(zhi[s], zlo[s], thi[kb], tlo[kb])
            for ci in range(2):
                for yl in range(2):
                    q = (ci * 2 + yl) * 128
                    V[s, zi, ci, yh * 2 + yl] = mo[:, q:q + 128].reshape(4, 64, 128)

            @pl.when(yh == 1)
            def _():
                sb_copy(s, zi).start()
        loop(0, 8, body)

    moment(0, [])

    def first():
        sib_add(0)
        rs_start(0, 0)

    moment(1, [(1, first), (4, lambda: rs_mid(0, 0)), (7, lambda: (rs_end(0, 0), rs_start(0, 1)) and None)])
    u_copy(2).wait_recv()
    u_copy(3).wait_recv()

    def mg_send(s):
        mg[s, c, y, z] = V[s, z, c, y, x]
        loop(1, 16, lambda k: mg_copy(s, k).start())

    def mg_wait(s):
        loop(1, 16, lambda k: mg_copy(s, k).wait_recv())
        mg_fwd(s).start()

    def rotate(s):
        mg_fwd(s).wait_recv()
        total = jnp.zeros((64, 128), F32)
        for kb in range(8):
            yh, zi = kb // 4, kb % 4
            lhs = jnp.concatenate([mg[s, ci, yh * 2 + yl, zi] for ci in range(2) for yl in range(2)], axis=1)
            lh, ll = split(lhs)
            cols = slice(kb * 512, (kb + 1) * 512)
            total = total + mm3(lh, ll, uhi[:, cols], ulo[:, cols], NT)
        et = eg[...].reshape(128, 128).T
        sh, sl = split(total / et[s * 64:(s + 1) * 64])
        for kb in range(8):
            yh, zi = kb // 4, kb % 4
            cols = slice(kb * 512, (kb + 1) * 512)
            part = mm3(sh, sl, uhi[:, cols], ulo[:, cols])
            for ci in range(2):
                for yl in range(2):
                    q = (ci * 2 + yl) * 128
                    ub[s, ci, yh * 2 + yl, zi] = part[:, q:q + 128]
        ub_sib(s).start()

    def ub_send(s):
        ub_sib(s).wait_recv()
        for yi in range(4):
            ub[s, c, yi] = ub[s, c, yi] + ubr[s, yi]
        loop(1, 16, lambda k: ub_copy(s, k).start())

    def ud_send(s):
        loop(1, 16, lambda k: ub_copy(s, k).wait_recv())
        total = ub[s, c, y, z]
        for k in range(1, 16):
            total = total + rb[s, k]
        ud[s, x, ylo] = total
        loop(1, 8, lambda k: ud_copy(s, k).start())

    sib_add(1)
    rs_start(1, 0)
    rs_mid(0, 1)
    for i in range(4):
        h, l = split(utg[i])
        uhi[i * 32:(i + 1) * 32, :] = h
        ulo[i * 32:(i + 1) * 32, :] = l
    for d in (1, 2, 3):
        e_copy(d).wait_recv()
    rs_end(0, 1)
    rs_start(0, 2)
    rs_mid(1, 0)
    rs_mid(0, 2)
    rs_end(0, 2)
    mg_send(0)
    rs_end(1, 0)
    rs_start(1, 1)
    mg_wait(0)
    rs_mid(1, 1)
    rs_end(1, 1)
    rs_start(1, 2)
    rotate(0)
    rs_mid(1, 2)
    rs_end(1, 2)
    mg_send(1)
    ub_send(0)
    mg_wait(1)
    rotate(1)
    ud_send(0)
    ub_send(1)
    oh, ol = split(outb[...])
    ud_send(1)
    loop(1, 8, lambda k: ud_copy(0, k).wait_recv())
    loop(1, 8, lambda k: ud_copy(1, k).wait_recv())
    cols = []
    for yl in range(2):
        cols.append(jnp.concatenate([ud[s, xi, yl] for xi in range(4) for s in range(2)], axis=0))
    dh, dl = split(jnp.concatenate(cols, axis=1))
    out[...] = mm3(oh, ol, dh, dl).T

    for k in range(4):
        u_copy(k).wait_send()
    for d in (1, 2, 3):
        e_copy(d).wait_send()
    for s in range(2):
        loop(0, 4, lambda zi: sb_copy(s, zi).wait_send())
        for o in range(3):
            for p in range(3):
                for k in range(4):
                    rs_copy(s, o, p, k).wait_send()
        mg_fwd(s).wait_send()
        ub_sib(s).wait_send()
        loop(1, 16, lambda k: mg_copy(s, k).wait_send())
        loop(1, 16, lambda k: ub_copy(s, k).wait_send())
        loop(1, 8, lambda k: ud_copy(s, k).wait_send())


def body(tokens, curvature, values, input_basis, output_basis, eigenvalues):
    inverse_total = 1.0 / (tokens.shape[0] * lax.axis_size("dp") * lax.axis_size("fsdp"))
    dma = pltpu.SemaphoreType.DMA
    scratch = [
        pltpu.VMEM((2, 4, 2, 4, 4, 64, 128), F32),
        pltpu.VMEM((8, 1024, 512), BF16),
        pltpu.VMEM((8, 1024, 512), BF16),
        pltpu.VMEM((2, 1024, 256), F32),
        pltpu.VMEM((1024, 512), F32),
        pltpu.VMEM((1024, 256), F32),
        pltpu.VMEM((1024, 512), BF16),
        pltpu.VMEM((1024, 512), BF16),
        pltpu.VMEM((2, 256, 1024), BF16),
        pltpu.VMEM((2, 256, 1024), BF16),
        pltpu.VMEM((2, 4, 4, 4, 64, 128), F32),
        pltpu.VMEM((2, 2, 4, 4, 64, 128), F32),
        pltpu.VMEM((4, 32, 4096), F32),
        pltpu.VMEM((128, 4096), BF16),
        pltpu.VMEM((128, 4096), BF16),
        pltpu.VMEM((4, 32, 128), F32),
        pltpu.VMEM((2, 2, 4, 4, 64, 128), F32),
        pltpu.VMEM((2, 4, 4, 64, 128), F32),
        pltpu.VMEM((2, 16, 64, 128), F32),
        pltpu.VMEM((2, 4, 2, 64, 128), F32),
    ]
    scratch += [pltpu.VMEM((2, 2) + half_shape(o, p), F32) for o in range(3) for p in range(3)]
    scratch += [pltpu.VMEM((2, 2) + full_shape(o, p), F32) for o in range(3) for p in range(3)]
    for n in (72, 72, 24, 24, 4, 4, 3, 3, 8, 8, 72, 72, 32, 32, 32, 32, 16, 16, 2, 4):
        scratch.append(dma((n,)))
    hbm = pl.BlockSpec(memory_space=pl.ANY)
    vmem = pl.BlockSpec(memory_space=pltpu.VMEM)
    update = pl.pallas_call(
        functools.partial(kernel, inverse_total=inverse_total),
        out_shape=jax.ShapeDtypeStruct((256, 512), F32),
        in_specs=[hbm, hbm, hbm, hbm, vmem, vmem, vmem],
        out_specs=vmem,
        scratch_shapes=scratch,
        compiler_params=pltpu.CompilerParams(
            collective_id=0, has_side_effects=True, vmem_limit_bytes=63 * 1024 * 1024
        ),
        cost_estimate=pl.CostEstimate(flops=30_000_000_000, bytes_accessed=24_000_000, transcendentals=0),
    )(
        tokens,
        curvature,
        values,
        input_basis.T,
        output_basis.T.reshape(4, 2, 64, 512),
        output_basis,
        eigenvalues,
    )
    return values - update


def solution(mesh):
    placed = (
        P(("dp", "fsdp"), None),
        P(("dp", "fsdp"), None),
        P("fsdp", None),
        P(None, ("dp", "fsdp")),
        P(),
        P(("dp", "fsdp"), None),
    )
    return jax.shard_map(
        body, mesh=mesh, in_specs=placed, out_specs=P("fsdp", None), check_vma=False
    )
```

time: 606 us -> 173 us (0.29)
  waiting for transfers between devices: 509 us -> 0 us
  Pallas kernels: 0 us -> 168 us
  matrix products: 80.8 us -> 0 us
  between operations: 13.6 us -> 0.02 us
    reduce_scatter x2 -> x0, waiting for transfers between devices: 200 us -> none  [the longest x1 100 us: body(): lax.psum_scatter(product * inverse_total, 'fsdp', scatter_dimension=0, ti...]
    pallas_call x0 -> x1, Pallas kernels: none -> 168 us  [body(): pl.pallas_call(functools.partial(kernel, inverse_total=inverse_total), ou...]
    all_gather x2 -> x0, waiting for transfers between devices: 157 us -> none  [the longest x1 79 us: body(): lax.all_gather(summed_rows, 'fsdp', axis=0, tiled=True)]
    psum x2 -> x0, waiting for transfers between devices: 151 us -> none  [the longest x1 75.6 us: body(): summed_rows = lax.psum(group_rows, 'dp')]
    dot_general x6 -> x0, matrix products: 80.8 us -> none  [the longest x1 31.3 us: body(): lax.dot_general(columns, weighted, (((0,), (0,)), ((), ())), precision=hi...]
  transfers between devices with their start and end apart: 6 -> 0, of which waited for: 6 -> 0; matrix products, arithmetic and copies ran while one was open for 0% -> 0% of each run, Pallas kernels for 0% -> 0%
where the time goes in v1:
time: 173 us; the launch traced here: 172 us
  Pallas kernels  168 us (97%)
  local copies, waits for them, and re-layouts  2.55 us (1%)
  other arithmetic  1.91 us (1%)
    pallas_call x1, Pallas kernels, body(): pl.pallas_call(functools.partial(kernel, inverse_total=inverse_total), ou...  168 us

profile of v1, /device:TPU:0, one launch (start us, length us, event | category | flops | bytes accessed | tf_op | source)
XLA Modules:
  0.0 172.3 jit_solution(3959589549414203549)
XLA Ops:
  0.0 2.5 %copy.7 = f32[512,512]{1,0:T(8,128)} copy(f32[512,512]{0,1:T(8,128)} %bitcast.3) | data formatting | bytes 2097152 | tf_op jit(solution)/shard_map/transpose | solution.py:583
  2.5 0.0 copy-start
  2.5 167.8 %shard_map.64 = f32[256,512]{1,0:T(8,128)} custom-call(f32[1024,4096]{1,0:T(8,128)} %tok.1, f32[1024,512]{1,0:T(8,128)} %curv.1, f32[256,512]{1,0:T(8,128)} %val.1, f32[32,4096]{1,0:T(8,128)} %bitcast.5, f32[4,2,64,512]{3,2,1,0:T(8,128)} %bitcast.4, f32[512,512]{1,0:T(8,128)} %outb.1, f32[32,512]{1,0:T(8,128)} %eig.1), custom_call_target="tpu_custom_call" | custom-call | flops 30000001024 | bytes 24000000 | tf_op jit(solution)/shard_map/pallas_call | solution.py:568
  170.4 0.0 copy-done
  170.4 1.9 %sub.3 = f32[256,512]{1,0:T(8,128)} subtract(f32[256,512]{1,0:T(8,128)S(1)} %copy-done, f32[256,512]{1,0:T(8,128)} %shard_map.64) | non-fusion elementwise | flops 131072 | bytes 1572864 | tf_op jit(solution)/shard_map/sub | solution.py:587
Async XLA Ops:
  2.5 167.8 %copy-start = (f32[256,512]{1,0:T(8,128)S(1)}, f32[256,512]{1,0:T(8,128)}, u32[]{:S(2)}) copy-start(f32[256,512]{1,0:T(8,128)} %val.1) | copy-start | bytes 1572868
